TPU v7x, 128 devices: a whole 4x4x4 slice. The times are simulated.
128 devices in a mesh: roll: 16 (over z, y_hi, core), kvh: 8 (over y_lo, x).
Axes of the slice: x: 4, y: 4 (y_hi: 2, y_lo: 2; y = y_hi * 2 + y_lo), z: 4, core: 2. Of those that a mesh axis runs over, the one named last changes fastest.
Arguments:
- out_grad: bfloat16 [16, 256, 5120], P('roll', 'kvh'), may hold values from -48 to 48
- out_weight: bfloat16 [8, 5, 128, 5120], P('kvh'), may hold values from -0.078125 to 0.078125
- queries: bfloat16 [16, 256, 8, 5, 128], P('roll', None, 'kvh'), may hold values from -16 to 16
- keys_new: bfloat16 [16, 256, 8, 128], P('roll', None, 'kvh'), may hold values from -16 to 16
- values_new: bfloat16 [16, 256, 8, 128], P('roll', None, 'kvh'), may hold values from -6 to 6
- keys_prompt: bfloat16 [4096, 8, 128], P('roll', 'kvh'), may hold values from -6 to 6
- values_prompt: bfloat16 [4096, 8, 128], P('roll', 'kvh'), may hold values from -6 to 6
- offsets: int32 [16], P('roll'), may hold values from 0 to 3840
Outputs:
- grad_queries: bfloat16 [16, 256, 8, 5, 128], P('roll', None, 'kvh')
- grad_keys_new: bfloat16 [16, 256, 8, 128], P('roll', None, 'kvh')
- grad_values_new: bfloat16 [16, 256, 8, 128], P('roll', None, 'kvh')
- grad_keys_prompt: bfloat16 [4096, 8, 128], P('roll', 'kvh')
- grad_values_prompt: bfloat16 [4096, 8, 128], P('roll', 'kvh')
Inputs may be any that keep to these rules, and one draw needn't show every extreme that they name: `offsets`: each slice lies inside a response of 4096 tokens.
All inputs are finite; a program needn't handle non-finite values.
Results may differ from a plain program's by a relative error of at most 0.015.
The roundings to bfloat16 on the way count: a program that leaves them out, or rounds other values in their place, can miss the bound.
Values may be sent and summed in bfloat16 or wider, within the bound.
A program may use at most 64 MiB of HBM per device.

v0:
```python
import math
import jax
import jax.numpy as jnp
from jax import lax
from jax.sharding import PartitionSpec as P

theta_base = 1000000.0


def rotation(positions, head_width):
    half_width = head_width // 2
    frequency = jnp.power(theta_base, -(jnp.arange(half_width, dtype=jnp.float32) / half_width))
    angles = positions.astype(jnp.float32)[:, None] * frequency[None, :]
    return (jnp.cos(angles), jnp.sin(angles))


def rotate(vectors, cos_part, sin_part, direction):
    half_width = vectors.shape[-1] // 2
    front_half = vectors[..., :half_width]
    back_half = vectors[..., half_width:]
    return jnp.concatenate(
        [
            front_half * cos_part - direction * back_half * sin_part,
            back_half * cos_part + direction * front_half * sin_part,
        ],
        axis=-1,
    )


def inner_dot(left, right):
    return lax.dot_general(
        left, right, (((1,), (1,)), ((), ())), preferred_element_type=jnp.float32
    )


def outer_sum(left, right):
    return lax.dot_general(
        left, right, (((0,), (0,)), ((), ())), preferred_element_type=jnp.float32
    )


def block_grads(context, key_block, value_block):
    query_rows, grad_rows, log_total, row_delta, score_scale = context
    scores = inner_dot(query_rows, key_block) * score_scale
    attn_probs = jnp.exp(scores - log_total[:, None]).astype(jnp.bfloat16)
    prob_grad = inner_dot(grad_rows, value_block)
    score_grad = (
        attn_probs.astype(jnp.float32) * (prob_grad - row_delta[:, None]) * score_scale
    ).astype(jnp.bfloat16)
    return (attn_probs, score_grad)


def local(out_grad, out_weight, queries, keys_new, values_new, keys_prompt, values_prompt, offsets):
    roll_local, seq_len, kv_local, group_size, head_width = queries.shape
    prompt_local = keys_prompt.shape[0]
    prompt_total = prompt_local * lax.axis_size("roll")
    score_scale = head_width ** (-0.5)
    row_total = roll_local * seq_len * group_size
    attn_grad = jnp.einsum(
        "rsc,ghdc->rsghd",
        lax.all_gather(out_grad, "kvh", axis=1, tiled=True),
        out_weight,
        preferred_element_type=jnp.float32,
    ).astype(jnp.bfloat16)
    cached_keys, cached_values = (
        lax.all_gather(keys_prompt, "roll", axis=0, tiled=True),
        lax.all_gather(values_prompt, "roll", axis=0, tiled=True),
    )
    positions = prompt_total + offsets[:, None] + jnp.arange(seq_len, dtype=jnp.int32)[None, :]
    cos_flat, sin_flat = rotation(positions.reshape(-1), head_width)
    cos_four = cos_flat.reshape(roll_local, seq_len, 1, head_width // 2)
    sin_four = sin_flat.reshape(roll_local, seq_len, 1, head_width // 2)
    query_rot = rotate(
        queries.astype(jnp.float32), cos_four[:, :, :, None], sin_four[:, :, :, None], 1.0
    ).astype(jnp.bfloat16)
    key_rot = rotate(keys_new.astype(jnp.float32), cos_four, sin_four, 1.0).astype(jnp.bfloat16)
    block_len = math.gcd(prompt_total, 512)
    block_count = prompt_total // block_len
    causal = (jnp.arange(seq_len)[None, :] <= jnp.arange(seq_len)[:, None])[None, :, None, :]
    contexts = []
    query_head = query_rot[:, :, 0]
    key_head = key_rot[:, :, 0]
    value_head = values_new[:, :, 0]
    grad_head = attn_grad[:, :, 0]
    query_rows = query_head.reshape(row_total, head_width)
    grad_rows = grad_head.reshape(row_total, head_width)
    key_blocks = cached_keys[:, 0].reshape(block_count, block_len, head_width)
    value_blocks = cached_values[:, 0].reshape(block_count, block_len, head_width)
    near_scores = (
        jnp.einsum("rshd,rtd->rsht", query_head, key_head, preferred_element_type=jnp.float32)
        * score_scale
    )
    near_scores = jnp.where(causal, near_scores, -jnp.inf)
    near_max = jnp.max(near_scores, axis=3, keepdims=True)
    near_sum = jnp.sum(jnp.exp(near_scores - near_max), axis=3)

    def stat_step(running, key_block):
        old_max, old_sum = running
        scores = inner_dot(query_rows, key_block) * score_scale
        new_max = jnp.maximum(old_max, jnp.max(scores, axis=1))
        new_sum = old_sum * jnp.exp(old_max - new_max) + jnp.sum(
            jnp.exp(scores - new_max[:, None]), axis=1
        )
        return ((new_max, new_sum), None)

    stats, unused = lax.scan(
        stat_step, (near_max.reshape(row_total), near_sum.reshape(row_total)), key_blocks
    )
    log_total = stats[0] + jnp.log(stats[1])
    log_shaped = log_total.reshape(roll_local, seq_len, group_size, 1)
    near_probs = jnp.where(causal, jnp.exp(near_scores - log_shaped), 0.0).astype(jnp.bfloat16)
    near_output = jnp.einsum(
        "rsht,rtd->rshd", near_probs, value_head, preferred_element_type=jnp.float32
    ).reshape(row_total, head_width)

    def output_step(total_out, blocks):
        scores = inner_dot(query_rows, blocks[0]) * score_scale
        attn_probs = jnp.exp(scores - log_total[:, None]).astype(jnp.bfloat16)
        return (
            total_out + jnp.dot(attn_probs, blocks[1], preferred_element_type=jnp.float32),
            None,
        )

    output, unused = lax.scan(output_step, near_output, (key_blocks, value_blocks))
    row_delta = jnp.sum(grad_rows.astype(jnp.float32) * output, axis=1)
    context = (query_rows, grad_rows, log_total, row_delta, score_scale)
    contexts.append(context)
    near_prob_grad = jnp.einsum(
        "rshd,rtd->rsht", grad_head, value_head, preferred_element_type=jnp.float32
    )
    delta_shaped = row_delta.reshape(roll_local, seq_len, group_size, 1)
    near_grad = (
        near_probs.astype(jnp.float32) * (near_prob_grad - delta_shaped) * score_scale
    ).astype(jnp.bfloat16)
    near_query = jnp.einsum(
        "rsht,rtd->rshd", near_grad, key_head, preferred_element_type=jnp.float32
    )
    key_new_grad = jnp.einsum(
        "rsht,rshd->rtd", near_grad, query_head, preferred_element_type=jnp.float32
    )
    value_new_grad = jnp.einsum(
        "rsht,rshd->rtd", near_probs, grad_head, preferred_element_type=jnp.float32
    )
    zero_rows = jnp.zeros((row_total, head_width), jnp.float32)

    def grad_step(total_grad, blocks):
        attn_probs, score_grad = block_grads(context, blocks[0], blocks[1])
        block_term = jnp.stack(
            [outer_sum(score_grad, query_rows), outer_sum(attn_probs, grad_rows)], axis=1
        )
        return (
            total_grad + jnp.dot(score_grad, blocks[0], preferred_element_type=jnp.float32),
            block_term,
        )

    far_query, block_terms = lax.scan(grad_step, zero_rows, (key_blocks, value_blocks))
    term_list = [block_terms.reshape(prompt_total, 2, head_width)]
    query_grad = far_query.reshape(roll_local, seq_len, group_size, head_width) + near_query
    query_list = [rotate(query_grad, cos_four, sin_four, -1.0).astype(jnp.bfloat16)]
    key_list = [
        rotate(key_new_grad, cos_four[:, :, 0], sin_four[:, :, 0], -1.0).astype(jnp.bfloat16)
    ]
    value_list = [value_new_grad.astype(jnp.bfloat16)]
    reduced = lax.psum_scatter(
        jnp.stack(term_list, axis=1).astype(jnp.bfloat16), "roll", scatter_dimension=0, tiled=True
    ).astype(jnp.float32)
    grad_queries = jnp.stack(query_list, axis=2)
    grad_keys_new = jnp.stack(key_list, axis=2)
    grad_values_new = jnp.stack(value_list, axis=2)
    return (
        grad_queries,
        grad_keys_new,
        grad_values_new,
        reduced[:, :, 0].astype(jnp.bfloat16),
        reduced[:, :, 1].astype(jnp.bfloat16),
    )


def solution(mesh):
    placed = (
        P("roll", "kvh", None),
        P("kvh", None, None, None),
        P("roll", None, "kvh", None, None),
        P("roll", None, "kvh", None),
        P("roll", None, "kvh", None),
        P("roll", "kvh", None),
        P("roll", "kvh", None),
        P("roll"),
    )
    return jax.shard_map(
        local,
        mesh=mesh,
        in_specs=placed,
        out_specs=(
            P("roll", None, "kvh", None, None),
            P("roll", None, "kvh", None),
            P("roll", None, "kvh", None),
            P("roll", "kvh", None),
            P("roll", "kvh", None),
        ),
        check_vma=False,
    )
```

profile of v0, /device:TPU:0, one launch (start us, length us, event | category | flops | bytes accessed | tf_op | source)
XLA Modules:
  0.0 288.3 jit_solution(14173419729338895202)
XLA Ops:
  19.1 38.9 %all-gather.4.cloned.1.call-done = bf16[4096,1,128]{2,0,1:T(8,128)(2,1)} async-done(((bf16[256,1,128]{2,0,1:T(8,128)(2,1)}), bf16[4096,1,128]{2,0,1:T(8,128)(2,1)}) %all-gather.4.cloned.1.call-update) | async-done | bytes 1048592 | tf_op jit(solution)/shard_map/all_gather | solution.py:66
  58.0 15.1 %while.35 = (s32[]{:T(128)}, f32[1280]{0:T(1024)S(1)}, f32[1280]{0:T(1024)S(1)}, bf16[8,512,128]{2,1,0:T(8,128)(2,1)}, bf16[1280,128]{1,0:T(8,128)(2,1)S(1)}, /*index=5*/s32[]{:T(128)}) while((s32[]{:T(128)}, f32[1280]{0:T(1024)S(1)}, f32[1280]{0:T(1024)S(1)}, bf16[8,512,128]{2,1,0:T(8,128)(2,1)}, bf16[1280,128]{1,0:T(8,128)(2,1)S(1)}, ...), condition=%wide.region_5.6_spmd, body=%wide.region_2.5_spmd.sunk | while | flops 170396160 | bytes 5768273 | solution.py:106
  76.6 27.6 %all-gather.6.cloned.1.call-done = bf16[4096,1,128]{2,0,1:T(8,128)(2,1)} async-done(((bf16[256,1,128]{2,0,1:T(8,128)(2,1)}), bf16[4096,1,128]{2,0,1:T(8,128)(2,1)}) %all-gather.6.cloned.1.call-update) | async-done | bytes 1048592 | tf_op jit(solution)/shard_map/all_gather | solution.py:67
  104.1 15.5 %while.36 = (s32[]{:T(128)}, f32[1280,128]{1,0:T(8,128)S(1)}, bf16[8,512,128]{2,1,0:T(8,128)(2,1)}, bf16[1280,128]{1,0:T(8,128)(2,1)S(1)}, f32[1280]{0:T(1024)S(1)}, /*index=5*/bf16[8,512,128]{2,1,0:T(8,128)(2,1)}, s32[]{:T(128)}) while((s32[]{:T(128)}, f32[1280,128]{1,0:T(8,128)S(1)}, bf16[8,512,128]{2,1,0:T(8,128)(2,1)}, ...), condition=%wide.region_7.8_spmd, body=%wide.region_6.7_spmd.sunk | while | flops 337674240 | bytes 1906773 | solution.py:124
  104.1 1.9 convolution_add_fusion.5
  106.0 1.9 convolution_add_fusion.5
  108.0 1.9 convolution_add_fusion.5
  109.9 1.9 convolution_add_fusion.5
  111.9 1.9 convolution_add_fusion.5
  113.8 1.9 convolution_add_fusion.5
  115.7 1.9 convolution_add_fusion.5
  117.7 1.9 convolution_add_fusion.5
  119.6 27.1 %all-gather.8.cloned.1.call-done = bf16[1,256,5120]{2,1,0:T(8,128)(2,1)} async-done(((bf16[1,32,5120]{2,1,0:T(8,128)(2,1)}), bf16[1,256,5120]{2,1,0:T(8,128)(2,1)}) %all-gather.8.cloned.1.call-update) | async-done | bytes 2621456 | tf_op jit(solution)/shard_map/all_gather | solution.py:61
  146.7 5.9 %fusion.41 = bf16[256,5,128]{2,0,1:T(8,128)(2,1)S(1)} fusion(bf16[1,5,128,5120]{3,2,1,0:T(8,128)(2,1)} %param.15, bf16[1,256,5120]{2,1,0:T(8,128)(2,1)} %all-gather.8.cloned.1.call-done), kind=kOutput, calls=%fused_computation.54 | convolution fusion | flops 1677885440 | bytes 9502720 | tf_op jit(solution)/shard_map/rsc,ghdc->rsghd/dot_general | solution.py:59
  155.1 51.2 %while.37 = (s32[]{:T(128)}, f32[1280,128]{1,0:T(8,128)S(1)}, bf16[8,512,2,128]{3,1,2,0:T(8,128)(2,1)}, bf16[8,512,128]{2,1,0:T(8,128)(2,1)}, bf16[1280,128]{1,0...) while((s32[]{:T(128)}, f32[1280,128]{1,0:T(8,128)S(1)}, ...), condition=%wide.region_10.11_spmd.clone, body=%wide.region_9.10_spmd.clone.sunk | while | flops 844955648 | bytes 11675791 | solution.py:156
  155.1 1.5 fusion.126
  157.1 1.5 fusion.127
  159.1 1.7 convolution_add_fusion.6
  163.5 1.5 fusion.127
  165.5 1.7 convolution_add_fusion.6
  169.9 1.5 fusion.127
  171.9 1.7 convolution_add_fusion.6
  174.3 1.5 fusion.126
  178.3 1.7 convolution_add_fusion.6
  184.7 1.7 convolution_add_fusion.6
  191.1 1.7 convolution_add_fusion.6
  197.5 1.7 convolution_add_fusion.6
  203.9 1.7 convolution_add_fusion.6
  206.3 3.1 %copy.68 = bf16[8,512,2,128]{3,1,0,2:T(8,128)(2,1)} copy(bf16[8,512,2,128]{3,1,2,0:T(8,128)(2,1)} %get-tuple-element.117) | data formatting | bytes 4194304 | tf_op jit(solution)/shard_map/convert_element_type | solution.py:165
  213.3 1.6 fusion.40
  216.9 63.3 %reduce-scatter.2.cloned.1.call-done = bf16[256,1,2,128]{3,0,2,1:T(8,128)(2,1)} async-done(((bf16[4096,1,2,128]{3,0,2,1:T(8,128)(2,1)}), bf16[256,1,2,128]{3,0,2,1:T(8,128)(2,1)}) %reduce-scatter.2.cloned.1.call-update) | async-done | bytes 131088 | tf_op jit(solution)/shard_map/reduce_scatter | solution.py:164
  280.3 1.5 slice_bitcast_fusion
  (153 shorter events, 67.7 us)
Async XLA Ops:
  7.2 68.0 %copy-start = (bf16[1,256,1,128]{3,1,2,0:T(8,128)(2,1)S(1)}, bf16[1,256,1,128]{3,1,2,0:T(8,128)(2,1)}, u32[]{:S(2)}) copy-start(bf16[1,256,1,128]{3,1,2,0:T(8,128)(2,1)} %param.18) | copy-start | bytes 196612
  7.2 50.8 %all-gather.4.cloned.1.call-start = ((), (), s32[]{:S(2)}) async-start(), calls=%async_computation.1 | async-start | bytes 1114112 | tf_op jit(solution)/shard_map/all_gather | solution.py:66
  7.9 96.2 %all-gather.6.cloned.1.call-start = ((), (), s32[]{:S(2)}) async-start(), calls=%async_computation.2 | async-start | bytes 1114112 | tf_op jit(solution)/shard_map/all_gather | solution.py:67
  8.7 138.0 %all-gather.8.cloned.1.call-start = ((), (), s32[]{:S(2)}) async-start(), calls=%async_computation.3 | async-start | bytes 2949120 | tf_op jit(solution)/shard_map/all_gather | solution.py:61
  9.4 270.9 %reduce-scatter.2.cloned.1.call-start = ((), (), s32[]{:S(2)}) async-start(), calls=%async_computation.4 | async-start | bytes 2228224 | tf_op jit(solution)/shard_map/reduce_scatter | solution.py:164
  14.7 3.0 %copy-start.1 = (bf16[1,256,1,5,64]{4,1,3,2,0:T(8,128)(2,1)}, bf16[1,256,1,5,64]{4,1,3,2,0:T(8,128)(2,1)S(1)}, u32[]{:S(2)}) copy-start(bf16[1,256,1,5,64]{4,1,3,2,0:T(8,128)(2,1)S(1)} %get-tuple-element.210) | copy-start | bytes 491524
  14.7 3.0 %copy-start.3 = (bf16[1,256,1,5,64]{4,1,3,2,0:T(8,128)(2,1)}, bf16[1,256,1,5,64]{4,1,3,2,0:T(8,128)(2,1)S(1)}, u32[]{:S(2)}) copy-start(bf16[1,256,1,5,64]{4,1,3,2,0:T(8,128)(2,1)S(1)} %get-tuple-element.211) | copy-start | bytes 491524
  14.7 2.4 copy-start.9
  17.1 1.8 copy-start.7
  17.7 1.2 copy-start.8
  152.6 57.2 %copy-start.5 = (bf16[256,5,128]{2,0,1:T(8,128)(2,1)}, bf16[256,5,128]{2,0,1:T(8,128)(2,1)S(1)}, u32[]{:S(2)}) copy-start(bf16[256,5,128]{2,0,1:T(8,128)(2,1)S(1)} %fusion.41) | copy-start | bytes 983044
  209.4 1.0 copy-start.2
  209.4 1.1 copy-start.4
  211.0 2.3 copy-start.10
  212.2 2.7 copy-start.11
  213.3 2.6 copy-start.6
Sparse Core Ops, SparseCore 0:
  10.5 47.4 all-gather.3
  60.4 43.6 all-gather.5
  105.8 40.8 all-gather.7
  209.6 70.6 reduce-scatter.1
where the time goes:
time: 289 us; the launch traced here: 288 us
  waiting for transfers between devices  159 us (55%)
  matrix products  83.2 us (29%)
  local copies, waits for them, and re-layouts  15.5 us (5%)
  other arithmetic  15.2 us (5%)
  between operations  14.7 us (5%)
    reduce_scatter x1, waiting for transfers between devices, local(): lax.psum_scatter(jnp.stack(term_list, axis=1).astype(jnp.bfloat16), 'roll...  63.3 us
    all_gather x1, waiting for transfers between devices, local(): lax.all_gather(keys_prompt, 'roll', axis=0, tiled=True)  38.9 us
    dot_general x24, matrix products, inner_dot(): lax.dot_general(left, right, (((1,), (1,)), ((), ())), preferred_element_...  35 us
    all_gather x1, waiting for transfers between devices, local(): lax.all_gather(values_prompt, 'roll', axis=0, tiled=True)  27.6 us
    all_gather x1, waiting for transfers between devices, local(): lax.all_gather(out_grad, 'kvh', axis=1, tiled=True)  27.1 us
    dot_general x8, matrix products, output_step(): jnp.dot(attn_probs, blocks[1], preferred_element_type=jnp.float32)  15.3 us
    dot_general x8, matrix products, grad_step(): jnp.dot(score_grad, blocks[0], preferred_element_type=jnp.float32)  13.5 us
    dot_general x16, matrix products, outer_sum(): lax.dot_general(left, right, (((0,), (0,)), ((), ())), preferred_element_...  8.1 us
  transfers between devices with their start and end apart: 4, of which 4 were waited for; matrix products, arithmetic and copies ran while one was open for 17% of the time, Pallas kernels for 0%

commit v1 on v0

--- a/solution.py
+++ b/solution.py
@@ -5,6 +5,15 @@
 from jax.sharding import PartitionSpec as P
 
 theta_base = 1000000.0
+step_on_records_here = lambda packet: jnp.concatenate(
+    lax.all_to_all(
+        jnp.stack(lax.psum(1, axis_name="kvh") * [packet], axis=0),
+        axis_name="kvh",
+        concat_axis=0,
+        split_axis=0,
+    ),
+    axis=1,
+)
 
 
 def rotation(positions, head_width):
@@ -58,7 +67,7 @@
     row_total = roll_local * seq_len * group_size
     attn_grad = jnp.einsum(
         "rsc,ghdc->rsghd",
-        lax.all_gather(out_grad, "kvh", axis=1, tiled=True),
+        step_on_records_here(out_grad),
         out_weight,
         preferred_element_type=jnp.float32,
     ).astype(jnp.bfloat16)

time: 289 us -> 277 us (0.958)
  waiting for transfers between devices: 159 us -> 140 us
  starting transfers between devices: 0.15 us -> 5.64 us
  local copies, waits for them, and re-layouts: 15.5 us -> 19.7 us
    all_gather x1 -> x0, waiting for transfers between devices: 27.1 us -> none  [local(): lax.all_gather(out_grad, 'kvh', axis=1, tiled=True)]
    all_gather x1, waiting for transfers between devices: 38.9 us -> 47.3 us  [local(): lax.all_gather(keys_prompt, 'roll', axis=0, tiled=True)]
    all_to_all x0 -> x1, starting transfers between devices: none -> 5.53 us  [lax.all_to_all(jnp.stack(lax.psum(1, axis_name='kvh') * [packet], axis=0)...]
    another operation x2 -> x3, local copies, waits for them, and re-layouts: 0.48 us -> 4.07 us  [the longest x1 2.8 us: jnp.stack(lax.psum(1, axis_name='kvh') * [packet], axis=0)]
  transfers between devices with their start and end apart: 4 -> 4, of which waited for: 4 -> 3; matrix products, arithmetic and copies ran while one was open for 17% -> 18% of each run, Pallas kernels for 0% -> 0%
where the time goes in v1:
time: 277 us; the launch traced here: 276 us
  waiting for transfers between devices  140 us (51%)
  matrix products  82 us (30%)
  local copies, waits for them, and re-layouts  19.7 us (7%)
  between operations  14.8 us (5%)
  other arithmetic  12.7 us (5%)
  starting transfers between devices  5.64 us (2%)
    reduce_scatter x1, waiting for transfers between devices, local(): lax.psum_scatter(jnp.stack(term_list, axis=1).astype(jnp.bfloat16), 'roll...  64 us
    all_gather x1, waiting for transfers between devices, local(): lax.all_gather(keys_prompt, 'roll', axis=0, tiled=True)  47.3 us
    dot_general x24, matrix products, inner_dot(): lax.dot_general(left, right, (((1,), (1,)), ((), ())), preferred_element_...  35 us
    all_gather x1, waiting for transfers between devices, local(): lax.all_gather(values_prompt, 'roll', axis=0, tiled=True)  27.6 us
    dot_general x8, matrix products, output_step(): jnp.dot(attn_probs, blocks[1], preferred_element_type=jnp.float32)  15.3 us
    dot_general x8, matrix products, grad_step(): jnp.dot(score_grad, blocks[0], preferred_element_type=jnp.float32)  13.4 us
    dot_general x16, matrix products, outer_sum(): lax.dot_general(left, right, (((0,), (0,)), ((), ())), preferred_element_...  8.11 us
    dot_general x1, matrix products, local(): jnp.einsum('rsc,ghdc->rsghd', step_on_records_here(out_grad), out_weight,...  5.89 us
  transfers between devices with their start and end apart: 4, of which 3 were waited for; matrix products, arithmetic and copies ran while one was open for 18% of the time, Pallas kernels for 0%

profile of v1, /device:TPU:0, one launch (start us, length us, event | category | flops | bytes accessed | tf_op | source)
XLA Modules:
  0.0 276.0 jit_solution(3768227934715048195)
XLA Ops:
  7.9 2.8 %stack.10 = bf16[8,1,32,5120]{3,2,1,0:T(8,128)(2,1)} broadcast(bf16[32,5120]{1,0:T(8,128)(2,1)} %bitcast.149), dimensions={2,3} | broadcast | bytes 2949120 | tf_op jit(solution)/shard_map/stack | solution.py:10
  10.7 5.5 %all-to-all-start = ((bf16[8,1,32,5120]{3,2,1,0:T(8,128)(2,1)}), bf16[8,1,32,5120]{3,2,1,0:T(8,128)(2,1)}, u32[]{:S(2)}, u32[]{:S(2)}) async-start(bf16[8,1,32,5120]{3,2,1,0:T(8,128)(2,1)} %stack.10), calls=%async_computation | async-start | bytes 5242880 | tf_op jit(solution)/shard_map/all_to_all | solution.py:9
  26.2 47.3 %all-gather.3.cloned.1.call-done = bf16[4096,1,128]{2,0,1:T(8,128)(2,1)} async-done(((bf16[256,1,128]{2,0,1:T(8,128)(2,1)}), bf16[4096,1,128]{2,0,1:T(8,128)(2,1)}) %all-gather.3.cloned.1.call-update) | async-done | bytes 1048592 | tf_op jit(solution)/shard_map/all_gather | solution.py:75
  73.5 15.1 %while.35 = (s32[]{:T(128)}, f32[1280]{0:T(1024)S(1)}, f32[1280]{0:T(1024)S(1)}, bf16[8,512,128]{2,1,0:T(8,128)(2,1)}, bf16[1280,128]{1,0:T(8,128)(2,1)S(1)}, /*index=5*/s32[]{:T(128)}) while((s32[]{:T(128)}, f32[1280]{0:T(1024)S(1)}, f32[1280]{0:T(1024)S(1)}, bf16[8,512,128]{2,1,0:T(8,128)(2,1)}, bf16[1280,128]{1,0:T(8,128)(2,1)S(1)}, ...), condition=%wide.region_5.6_spmd, body=%wide.region_2.5_spmd.sunk | while | flops 170396160 | bytes 5768773 | solution.py:115
  92.1 27.6 %all-gather.5.cloned.1.call-done = bf16[4096,1,128]{2,0,1:T(8,128)(2,1)} async-done(((bf16[256,1,128]{2,0,1:T(8,128)(2,1)}), bf16[4096,1,128]{2,0,1:T(8,128)(2,1)}) %all-gather.5.cloned.1.call-update) | async-done | bytes 1048592 | tf_op jit(solution)/shard_map/all_gather | solution.py:76
  119.7 15.5 %while.36 = (s32[]{:T(128)}, f32[1280,128]{1,0:T(8,128)S(1)}, bf16[8,512,128]{2,1,0:T(8,128)(2,1)}, bf16[1280,128]{1,0:T(8,128)(2,1)S(1)}, f32[1280]{0:T(1024)S(1)}, /*index=5*/bf16[8,512,128]{2,1,0:T(8,128)(2,1)}, s32[]{:T(128)}) while((s32[]{:T(128)}, f32[1280,128]{1,0:T(8,128)S(1)}, bf16[8,512,128]{2,1,0:T(8,128)(2,1)}, ...), condition=%wide.region_7.8_spmd, body=%wide.region_6.7_spmd.sunk | while | flops 337674240 | bytes 1906765 | solution.py:133
  119.7 1.9 convolution_add_fusion.5
  121.6 1.9 convolution_add_fusion.5
  123.5 1.9 convolution_add_fusion.5
  125.5 1.9 convolution_add_fusion.5
  127.4 1.9 convolution_add_fusion.5
  129.4 1.9 convolution_add_fusion.5
  131.3 1.9 convolution_add_fusion.5
  133.2 1.9 convolution_add_fusion.5
  135.2 5.9 %fusion.40 = bf16[256,5,128]{2,0,1:T(8,128)(2,1)S(1)} fusion(bf16[256,5120,1]{1,0,2:T(8,128)(2,1)} %bitcast.13, bf16[1,5,128,5120]{3,2,1,0:T(8,128)(2,1)} %param.15), kind=kOutput, calls=%fused_computation.53 | convolution fusion | flops 1677885440 | bytes 9502720 | tf_op jit(solution)/shard_map/rsc,ghdc->rsghd/dot_general | solution.py:68
  143.6 51.3 %while.37 = (s32[]{:T(128)}, f32[1280,128]{1,0:T(8,128)S(1)}, bf16[8,512,2,128]{3,1,2,0:T(8,128)(2,1)}, bf16[8,512,128]{2,1,0:T(8,128)(2,1)}, bf16[1280,128]{1,0...) while((s32[]{:T(128)}, f32[1280,128]{1,0:T(8,128)S(1)}, ...), condition=%wide.region_10.11_spmd.clone, body=%wide.region_9.10_spmd.clone.sunk | while | flops 844955648 | bytes 11677815 | solution.py:165
  148.3 1.7 convolution_add_fusion.6
  154.7 1.7 convolution_add_fusion.6
  156.4 1.5 fusion.124
  161.1 1.7 convolution_add_fusion.6
  162.8 1.5 fusion.124
  167.5 1.7 convolution_add_fusion.6
  169.2 1.5 fusion.124
  173.9 1.7 convolution_add_fusion.6
  180.4 1.7 convolution_add_fusion.6
  186.8 1.7 convolution_add_fusion.6
  188.5 1.5 fusion.124
  189.9 1.5 fusion.125
  193.2 1.7 convolution_add_fusion.6
  194.9 3.1 %copy.68 = bf16[8,512,2,128]{3,1,0,2:T(8,128)(2,1)} copy(bf16[8,512,2,128]{3,1,2,0:T(8,128)(2,1)} %get-tuple-element.117) | data formatting | bytes 4194304 | tf_op jit(solution)/shard_map/convert_element_type | solution.py:174
  203.9 64.0 %reduce-scatter.2.cloned.1.call-done = bf16[256,1,2,128]{3,0,2,1:T(8,128)(2,1)} async-done(((bf16[4096,1,2,128]{3,0,2,1:T(8,128)(2,1)}), bf16[256,1,2,128]{3,0,2,1:T(8,128)(2,1)}) %reduce-scatter.2.cloned.1.call-update) | async-done | bytes 131088 | tf_op jit(solution)/shard_map/reduce_scatter | solution.py:173
  267.9 1.5 slice_bitcast_fusion
  (163 shorter events, 66.4 us)
Async XLA Ops:
  7.2 83.5 %copy-start = (bf16[1,256,1,128]{3,1,2,0:T(8,128)(2,1)S(1)}, bf16[1,256,1,128]{3,1,2,0:T(8,128)(2,1)}, u32[]{:S(2)}) copy-start(bf16[1,256,1,128]{3,1,2,0:T(8,128)(2,1)} %param.18) | copy-start | bytes 196612
  7.2 66.4 %all-gather.3.cloned.1.call-start = ((), (), s32[]{:S(2)}) async-start(), calls=%async_computation.2 | async-start | bytes 1114112 | tf_op jit(solution)/shard_map/all_gather | solution.py:75
  10.7 8.2 %copy-start.10 = (bf16[1,256,1,5,128]{4,1,3,2,0:T(8,128)(2,1)S(1)}, bf16[1,256,1,5,128]{4,1,3,2,0:T(8,128)(2,1)}, u32[]{:S(2)}) copy-start(bf16[1,256,1,5,128]{4,1,3,2,0:T(8,128)(2,1)} %param.16) | copy-start | bytes 983044
  10.7 8.3 %copy-start.12 = (bf16[1,256,1,128]{3,1,2,0:T(8,128)(2,1)S(1)}, bf16[1,256,1,128]{3,1,2,0:T(8,128)(2,1)}, u32[]{:S(2)}) copy-start(bf16[1,256,1,128]{3,1,2,0:T(8,128)(2,1)} %param.17) | copy-start | bytes 196612
  10.7 124.4 %all-to-all-start = ((bf16[8,1,32,5120]{3,2,1,0:T(8,128)(2,1)}), bf16[8,1,32,5120]{3,2,1,0:T(8,128)(2,1)}, u32[]{:S(2)}, u32[]{:S(2)}) async-start(bf16[8,1,32,5120]{3,2,1,0:T(8,128)(2,1)} %stack.10), calls=%async_computation | async-start | bytes 5242880 | tf_op jit(solution)/shard_map/all_to_all | solution.py:9
  16.2 103.4 %all-gather.5.cloned.1.call-start = ((), (), s32[]{:S(2)}) async-start(), calls=%async_computation.3 | async-start | bytes 1114112 | tf_op jit(solution)/shard_map/all_gather | solution.py:76
  17.0 250.9 %reduce-scatter.2.cloned.1.call-start = ((), (), s32[]{:S(2)}) async-start(), calls=%async_computation.4 | async-start | bytes 2228224 | tf_op jit(solution)/shard_map/reduce_scatter | solution.py:173
  17.1 2.9 %copy-start.15 = (f32[64]{0:T(128)}, f32[64]{0:T(128)S(1)}, u32[]{:S(2)}) copy-start(f32[64]{0:T(128)S(1)} %negate_power_fusion) | copy-start | bytes 772
  17.8 2.2 copy-start.13
  19.6 2.2 copy-start.8
  19.9 3.1 %copy-start.1 = (bf16[1,256,1,5,64]{4,1,3,2,0:T(8,128)(2,1)}, bf16[1,256,1,5,64]{4,1,3,2,0:T(8,128)(2,1)S(1)}, u32[]{:S(2)}) copy-start(bf16[1,256,1,5,64]{4,1,3,2,0:T(8,128)(2,1)S(1)} %get-tuple-element.210) | copy-start | bytes 491524
  20.0 3.1 %copy-start.3 = (bf16[1,256,1,5,64]{4,1,3,2,0:T(8,128)(2,1)}, bf16[1,256,1,5,64]{4,1,3,2,0:T(8,128)(2,1)S(1)}, u32[]{:S(2)}) copy-start(bf16[1,256,1,5,64]{4,1,3,2,0:T(8,128)(2,1)S(1)} %get-tuple-element.211) | copy-start | bytes 491524
  141.1 2.5 copy-start.5
  198.0 1.0 copy-start.6
  198.0 1.3 copy-start.2
  198.0 1.4 copy-start.4
  198.0 1.8 copy-start.14
  198.0 1.8 copy-start.16
  199.8 1.5 copy-start.9
  201.0 0.8 copy-start.11
  201.4 1.5 copy-start.7
Sparse Core Ops, SparseCore 0:
  10.5 63.0 all-gather.2
  76.0 43.6 all-gather.4
  198.1 69.7 reduce-scatter.1
